TPU v7x, 512 devices: a whole 4x4x16 slice. The times are simulated.
512 devices in a mesh: pair: 128 (over x, z, y_hi), occ: 4 (over y_lo, core).
Axes of the slice: x: 4, y: 4 (y_hi: 2, y_lo: 2; y = y_hi * 2 + y_lo), z: 16, core: 2. Of those that a mesh axis runs over, the one named last changes fastest.
Arguments:
- amplitudes: bfloat16 [128, 768, 4096], P('pair', 'occ'), may hold values from -6 to 6
- integrals: bfloat16 [128, 4096, 512], P('pair', 'occ'), may hold values from -0.03125 to 0.03125
- block_mask: int32 [128], P('pair'), may hold values 0 or 1
Outputs:
- ladder: float32 [768, 512], P('pair', 'occ')
All inputs are finite; a program needn't handle non-finite values. No bound on the sum of `block_mask` on one device may be relied on, other than what follows from the above.
Results may differ from a plain program's by a relative error of at most 0.0003.
Values may be sent and summed in bfloat16 or wider, within the bound.
No kernel may reach another device: no remote copies, remote signals or barrier semaphores. Data moves between devices by JAX's collectives and lax.ppermute only.
A program may use at most 64 MiB of HBM per device.

v0:
```python
import jax
import jax.numpy as jnp
from jax import lax
from jax.experimental import pallas as pl
from jax.experimental.pallas import tpu as pltpu
from jax.sharding import Mesh
from jax.sharding import PartitionSpec as P

NX, NZ, NYH, NYL, NC = 4, 16, 2, 2, 2
PAIR = ("x", "z", "yh")
OCC = ("yl", "core")
SWAP = [(0, 1), (1, 0)]
VMEM = pl.BlockSpec(memory_space=pltpu.VMEM)
SMEM = pl.BlockSpec(memory_space=pltpu.SMEM)
HBM = pl.BlockSpec(memory_space=pltpu.HBM)
DMA = pltpu.SemaphoreType.DMA


def call(kernel, out_shape, in_specs, scratch=(), flops=0, moved=0):
    return pl.pallas_call(
        kernel,
        out_shape=out_shape,
        in_specs=in_specs,
        out_specs=jax.tree.map(lambda _: VMEM, out_shape),
        scratch_shapes=list(scratch),
        compiler_params=pltpu.CompilerParams(vmem_limit_bytes=32 * 2**20),
        cost_estimate=pl.CostEstimate(flops=flops, bytes_accessed=moved, transcendentals=0),
    )


def take_half(amp, out, token, sem):
    half = out.shape[1]
    offset = pl.multiple_of((1 - lax.axis_index("yl")) * half, half)
    copy = pltpu.make_async_copy(amp.at[0, :, pl.ds(offset, half)], out, sem)
    copy.start()
    token[...] = jnp.zeros_like(token)
    copy.wait()


def take_late(sib_low, sib_high, early, away, out):
    del sib_low, sib_high, early
    out[...] = away[...]


def part_rows(token, integ, low, high):
    del token
    half = low.shape[0]
    low[...] = integ[:half]
    high[...] = integ[half:]


def spread(mask, a, columns, acc, out):
    acc[...] = mask[0].astype(jnp.float32) * jnp.dot(a[...], columns[...], preferred_element_type=jnp.float32)
    rows, width = out.shape[3:]
    own = rows // NZ
    for core in range(NC):
        for yh in range(NYH):
            for yl in range(NYL):
                left = (yl * NC + core) * width
                for z in range(NZ):
                    start = (z * NYH + yh) * own
                    out[core, yh, yl, z * own : (z + 1) * own] = acc[start : start + own, left : left + width]


def home_kernel(mask, amp, own_low, own_high, sib_low, sib_high, out, columns, half_ref, acc, sem):
    half = half_ref.shape[1]
    yl, core = lax.axis_index("yl"), lax.axis_index("core")
    offset = pl.multiple_of(yl * half, half)
    copy = pltpu.make_async_copy(amp.at[0, :, pl.ds(offset, half)], half_ref, sem)
    copy.start()
    depth = own_low.shape[0]
    for place, low, high in ((core, own_low, own_high), (1 - core, sib_low, sib_high)):
        first = pl.multiple_of(place * 2 * depth, 2 * depth)
        columns[pl.ds(first, depth)] = low[...]
        columns[pl.ds(first + depth, depth)] = high[...]
    copy.wait()
    spread(mask, half_ref, columns, acc, out)


def guest_kernel(mask, early, late, columns, home, out, acc):
    yl, core = lax.axis_index("yl"), lax.axis_index("core")
    out[yl] = home[...]

    @pl.when(core == 0)
    def _():
        spread(mask, early, columns, acc, out.at[1 - yl])

    @pl.when(core == 1)
    def _():
        spread(mask, late, columns, acc, out.at[1 - yl])


def per_device(amplitudes, integrals, block_mask):
    rows, depth = amplitudes.shape[1:]
    half = depth // NYL
    own = rows // (NZ * NYH)
    width = integrals.shape[2] // (NYL * NC)

    away, token = call(
        take_half,
        (
            jax.ShapeDtypeStruct((rows, half), jnp.bfloat16),
            jax.ShapeDtypeStruct((8, 128), jnp.float32),
        ),
        [HBM],
        [DMA],
        moved=4 * rows * half,
    )(amplitudes)
    early = lax.ppermute(away, OCC, [(0, 2), (2, 0)])
    depth_own, width_all = integrals.shape[1:]
    some_rows = jax.ShapeDtypeStruct((depth_own // 2, width_all), jnp.bfloat16)
    own_low, own_high = call(part_rows, (some_rows, some_rows), [VMEM, VMEM], moved=2**21)(
        token, integrals[0]
    )
    sib_low = lax.ppermute(own_low, "core", SWAP)
    sib_high = lax.ppermute(own_high, "core", SWAP)
    piece = jax.ShapeDtypeStruct((NC, NYH, NYL, rows // NYH, width), jnp.float32)
    acc = pltpu.VMEM((rows, width_all), jnp.float32)
    columns = jax.ShapeDtypeStruct((half, width_all), jnp.bfloat16)
    home, all_columns = call(
        home_kernel,
        (piece, columns),
        [SMEM, HBM] + [VMEM] * 4,
        [pltpu.VMEM((rows, half), jnp.bfloat16), acc, DMA],
        flops=1,
        moved=1,
    )(block_mask, amplitudes, own_low, own_high, sib_low, sib_high)
    away_late = call(
        take_late, jax.ShapeDtypeStruct((rows, half), jnp.bfloat16), [VMEM] * 4, moved=1
    )(sib_low, sib_high, early, away)
    late = lax.ppermute(away_late, OCC, [(1, 3), (3, 1)])

    parts = call(
        guest_kernel,
        jax.ShapeDtypeStruct((2,) + piece.shape, jnp.float32),
        [SMEM] + [VMEM] * 4,
        [acc],
        flops=2 * rows * half * width_all,
        moved=2**22,
    )(block_mask, early, late, all_columns, home)
    parts = parts.reshape(NX * NYH * NYL, rows // NYH, width)
    parts = lax.all_to_all(parts, ("x", "yh", "yl"), split_axis=0, concat_axis=0, tiled=True)
    plane = jnp.sum(parts, axis=0).reshape(NZ, own, width)
    plane = lax.all_to_all(plane, "z", split_axis=0, concat_axis=0, tiled=True)
    block = jnp.sum(plane, axis=0)
    swap = [((h * 2 + b) * NC + c, (h * 2 + c) * NC + b) for h in range(2) for b in range(2) for c in range(NC)]
    return lax.ppermute(block, ("x", "core"), swap)


def solution(mesh):
    fine = Mesh(mesh.devices.reshape(NX, NZ, NYH, NYL, NC), PAIR + OCC)
    in_specs = (P(PAIR, OCC, None), P(PAIR, OCC, None), P(PAIR))
    return jax.shard_map(
        per_device, mesh=fine, in_specs=in_specs, out_specs=P(PAIR, OCC), check_vma=False
    )
```

profile of v0, /device:TPU:1, one launch (start us, length us, event | category | flops | bytes accessed | tf_op | source)
XLA Modules:
  0.0 74.5 jit_solution(10822797988419432854)
XLA Ops:
  0.0 0.0 copy-start
  0.0 1.4 %copy-done = bf16[1,192,4096]{2,1,0:T(8,128)(2,1)S(1)} copy-done((bf16[1,192,4096]{2,1,0:T(8,128)(2,1)S(1)}, bf16[1,192,4096]{2,1,0:T(8,128)(2,1)}, u32[]{:S(2)}) %copy-start) | copy-done | bytes 1572888
  1.4 0.0 copy-start.2
  1.4 0.1 shard_map.37
  1.5 0.8 %collective-permute-start = (bf16[192,2048]{1,0:T(8,128)(2,1)S(1)}, bf16[192,2048]{1,0:T(8,128)(2,1)S(1)}, u32[]{:S(2)}, u32[]{:S(2)}) collective-permute-start(bf16[192,2048]{1,0:T(8,128)(2,1)S(1)} %get-tuple-element.11.away), channel_id=1, source_target_pairs={{0,2},{2,0},{4,6},{6,4},{8,10},{10,8},{12,14},{14,12},{16,18},{18,... | collective-permute-start | bytes 2359304 | tf_op jit(solution)/shard_map/ppermute | solution.py:109
  2.4 0.3 copy-done.2
  2.6 0.0 copy-start.1
  2.6 0.1 shard_map.38
  2.7 9.9 %collective-permute-start.1 = (bf16[512,512]{1,0:T(8,128)(2,1)S(1)}, bf16[512,512]{1,0:T(8,128)(2,1)S(1)}, u32[]{:S(2)}, u32[]{:S(2)}) collective-permute-start(bf16[512,512]{1,0:T(8,128)(2,1)S(1)} %get-tuple-element.13.own_low), channel_id=1, source_target_pairs={{0,1},{1,0},{2,3},{3,2},{4,5},{5,4},{6,7},{7,6},{8,9},{9,8},{10,11... | collective-permute-start | bytes 1572872 | tf_op jit(solution)/shard_map/ppermute | solution.py:115
  12.6 1.9 %collective-permute-start.2 = (bf16[512,512]{1,0:T(8,128)(2,1)S(1)}, bf16[512,512]{1,0:T(8,128)(2,1)S(1)}, u32[]{:S(2)}, u32[]{:S(2)}) collective-permute-start(bf16[512,512]{1,0:T(8,128)(2,1)S(1)} %get-tuple-element.14.own_high), channel_id=1, source_target_pairs={{0,1},{1,0},{2,3},{3,2},{4,5},{5,4},{6,7},{7,6},{8,9},{9,8},{10,11... | collective-permute-start | bytes 1572872 | tf_op jit(solution)/shard_map/ppermute | solution.py:116
  14.5 0.0 collective-permute-done.1.sib_low
  14.5 1.9 %collective-permute-done.2.sib_high = bf16[512,512]{1,0:T(8,128)(2,1)S(1)} collective-permute-done((bf16[512,512]{1,0:T(8,128)(2,1)S(1)}, bf16[512,512]{1,0:T(8,128)(2,1)S(1)}, u32[]{:S(2)}, u32[]{:S(2)}) %collective-permute-start.2) | collective-permute-done | bytes 524320 | tf_op jit(solution)/shard_map/ppermute | solution.py:116
  16.4 0.0 collective-permute-done.early
  16.4 0.1 shard_map.39
  16.5 3.6 %collective-permute-start.3 = (bf16[192,2048]{1,0:T(8,128)(2,1)S(1)}, bf16[192,2048]{1,0:T(8,128)(2,1)S(1)}, u32[]{:S(2)}, u32[]{:S(2)}) collective-permute-start(bf16[192,2048]{1,0:T(8,128)(2,1)S(1)} %shard_map.39), channel_id=1, source_target_pairs={{1,3},{3,1},{5,7},{7,5},{9,11},{11,9},{13,15},{15,13},{17,19},{19,... | collective-permute-start | bytes 2359304 | tf_op jit(solution)/shard_map/ppermute | solution.py:131
  20.8 0.0 copy-done.1
  20.8 0.9 %shard_map.40 = (f32[2,2,2,96,128]{4,3,2,1,0:T(8,128)S(1)}, bf16[2048,512]{1,0:T(8,128)(2,1)S(1)}) custom-call(s32[1]{0:T(128)S(6)} %copy.5.mask, bf16[1,192,4096]{2,1,0:T(8,128)(2,1)S(1)} %copy-done.1, bf16[512,512]{1,0:T(8,128)(2,1)S(1)} %get-tuple-element.13.own_low, bf16[512,512]{1,0:T(8,128)(2,1)S(1)} %get-tuple-element.14.own_high, ...), custom_call_target="tpu_custom_call" | custom-call | flops 1 | bytes 1 | tf_op jit(solution)/shard_map/pallas_call | solution.py:120
  21.7 8.5 %collective-permute-done.3.late = bf16[192,2048]{1,0:T(8,128)(2,1)S(1)} collective-permute-done((bf16[192,2048]{1,0:T(8,128)(2,1)S(1)}, bf16[192,2048]{1,0:T(8,128)(2,1)S(1)}, u32[]{:S(2)}, u32[]{:S(2)}) %collective-permute-start.3) | collective-permute-done | bytes 786464 | tf_op jit(solution)/shard_map/ppermute | solution.py:131
  30.1 0.7 shard_map.41
  30.8 12.8 %all_to_all.10 = f32[16,96,128]{2,1,0:T(8,128)S(1)} all-to-all(f32[16,96,128]{2,1,0:T(8,128)S(1)} %bitcast.2), channel_id=1, replica_groups=mesh['x'=4,'z'=16,'yh'=2,'yl'=2,'core'=2] {'x','yh','yl'}, dimensions={0} | all-to-all | bytes 1572864 | tf_op jit(solution)/shard_map/all_to_all | solution.py:142
  43.6 25.3 %all_to_all.11 = f32[16,6,128]{2,1,0:T(8,128)S(1)} all-to-all(f32[16,6,128]{2,1,0:T(8,128)S(1)} %reshape.7), channel_id=1, replica_groups=mesh['x'=4,'z'=16,'yh'=2,'yl'=2,'core'=2] {'z'}, dimensions={0} | all-to-all | bytes 98304 | tf_op jit(solution)/shard_map/all_to_all | solution.py:144
  69.0 1.9 %collective-permute-start.4 = (f32[6,128]{1,0:T(8,128)S(1)}, f32[6,128]{1,0:T(8,128)S(1)}, u32[]{:S(2)}, u32[]{:S(2)}) collective-permute-start(f32[6,128]{1,0:T(8,128)S(1)} %reduce_sum.19), channel_id=1, source_target_pairs={{0,0},{1,128},{128,1},{129,129},{256,256},{257,384},{384,257},{385... | collective-permute-start | bytes 9224 | tf_op jit(solution)/shard_map/ppermute | solution.py:147
  70.9 3.0 %collective-permute-done.4 = f32[6,128]{1,0:T(8,128)S(1)} collective-permute-done((f32[6,128]{1,0:T(8,128)S(1)}, f32[6,128]{1,0:T(8,128)S(1)}, u32[]{:S(2)}, u32[]{:S(2)}) %collective-permute-start.4) | collective-permute-done | bytes 3104 | tf_op jit(solution)/shard_map/ppermute | solution.py:147
  73.9 0.6 copy.6
  (3 shorter events, 0.1 us)
Async XLA Ops:
  0.0 1.4 %copy-start = (bf16[1,192,4096]{2,1,0:T(8,128)(2,1)S(1)}, bf16[1,192,4096]{2,1,0:T(8,128)(2,1)}, u32[]{:S(2)}) copy-start(bf16[1,192,4096]{2,1,0:T(8,128)(2,1)} %amp.3) | copy-start | bytes 4718596
  1.4 1.2 %copy-start.2 = (bf16[1,1024,512]{2,1,0:T(8,128)(2,1)S(1)}, bf16[1,1024,512]{2,1,0:T(8,128)(2,1)}, u32[]{:S(2)}) copy-start(bf16[1,1024,512]{2,1,0:T(8,128)(2,1)} %param.4) | copy-start | bytes 3145732
  1.5 14.9 %collective-permute-start = (bf16[192,2048]{1,0:T(8,128)(2,1)S(1)}, bf16[192,2048]{1,0:T(8,128)(2,1)S(1)}, u32[]{:S(2)}, u32[]{:S(2)}) collective-permute-start(bf16[192,2048]{1,0:T(8,128)(2,1)S(1)} %get-tuple-element.11.away), channel_id=1, source_target_pairs={{0,2},{2,0},{4,6},{6,4},{8,10},{10,8},{12,14},{14,12},{16,18},{18,... | collective-permute-start | bytes 2359304 | tf_op jit(solution)/shard_map/ppermute | solution.py:109
  2.6 18.1 %copy-start.1 = (bf16[1,192,4096]{2,1,0:T(8,128)(2,1)S(1)}, bf16[1,192,4096]{2,1,0:T(8,128)(2,1)}, u32[]{:S(2)}) copy-start(bf16[1,192,4096]{2,1,0:T(8,128)(2,1)} %amp.3) | copy-start | bytes 4718596
  2.7 11.8 %collective-permute-start.1 = (bf16[512,512]{1,0:T(8,128)(2,1)S(1)}, bf16[512,512]{1,0:T(8,128)(2,1)S(1)}, u32[]{:S(2)}, u32[]{:S(2)}) collective-permute-start(bf16[512,512]{1,0:T(8,128)(2,1)S(1)} %get-tuple-element.13.own_low), channel_id=1, source_target_pairs={{0,1},{1,0},{2,3},{3,2},{4,5},{5,4},{6,7},{7,6},{8,9},{9,8},{10,11... | collective-permute-start | bytes 1572872 | tf_op jit(solution)/shard_map/ppermute | solution.py:115
  12.6 3.8 %collective-permute-start.2 = (bf16[512,512]{1,0:T(8,128)(2,1)S(1)}, bf16[512,512]{1,0:T(8,128)(2,1)S(1)}, u32[]{:S(2)}, u32[]{:S(2)}) collective-permute-start(bf16[512,512]{1,0:T(8,128)(2,1)S(1)} %get-tuple-element.14.own_high), channel_id=1, source_target_pairs={{0,1},{1,0},{2,3},{3,2},{4,5},{5,4},{6,7},{7,6},{8,9},{9,8},{10,11... | collective-permute-start | bytes 1572872 | tf_op jit(solution)/shard_map/ppermute | solution.py:116
  16.5 13.7 %collective-permute-start.3 = (bf16[192,2048]{1,0:T(8,128)(2,1)S(1)}, bf16[192,2048]{1,0:T(8,128)(2,1)S(1)}, u32[]{:S(2)}, u32[]{:S(2)}) collective-permute-start(bf16[192,2048]{1,0:T(8,128)(2,1)S(1)} %shard_map.39), channel_id=1, source_target_pairs={{1,3},{3,1},{5,7},{7,5},{9,11},{11,9},{13,15},{15,13},{17,19},{19,... | collective-permute-start | bytes 2359304 | tf_op jit(solution)/shard_map/ppermute | solution.py:131
  69.0 4.9 %collective-permute-start.4 = (f32[6,128]{1,0:T(8,128)S(1)}, f32[6,128]{1,0:T(8,128)S(1)}, u32[]{:S(2)}, u32[]{:S(2)}) collective-permute-start(f32[6,128]{1,0:T(8,128)S(1)} %reduce_sum.19), channel_id=1, source_target_pairs={{0,0},{1,128},{128,1},{129,129},{256,256},{257,384},{384,257},{385... | collective-permute-start | bytes 9224 | tf_op jit(solution)/shard_map/ppermute | solution.py:147
where the time goes:
time: 74.8 us; the launch traced here: 74.5 us
  blocking collectives  38.1 us (51%)
  starting transfers between devices  18.2 us (24%)
  waiting for transfers between devices  13.3 us (18%)
  local copies, waits for them, and re-layouts  2.28 us (3%)
  Pallas kernels  1.77 us (2%)
  between operations  0.75 us (1%)
    all_to_all x1, blocking collectives, per_device(): plane = lax.all_to_all(plane, 'z', split_axis=0, concat_axis=0, tiled=True)  25.3 us
    all_to_all x1, blocking collectives, per_device(): lax.all_to_all(parts, ('x', 'yh', 'yl'), split_axis=0, concat_axis=0, til...  12.8 us
    ppermute x1, starting transfers between devices, per_device(): sib_low = lax.ppermute(own_low, 'core', SWAP)  9.88 us
    ppermute x1, waiting for transfers between devices, per_device(): late = lax.ppermute(away_late, OCC, [(1, 3), (3, 1)])  8.48 us
    ppermute x1, starting transfers between devices, per_device(): late = lax.ppermute(away_late, OCC, [(1, 3), (3, 1)])  3.64 us
    ppermute x1, waiting for transfers between devices, per_device(): return lax.ppermute(block, ('x', 'core'), swap)  3 us
    unnamed x7, local copies, waits for them, and re-layouts  2.28 us
    ppermute x1, starting transfers between devices, per_device(): sib_high = lax.ppermute(own_high, 'core', SWAP)  1.92 us
  transfers between devices with their start and end apart: 5, of which 3 were waited for; matrix products, arithmetic and copies ran while one was open for 0% of the time, Pallas kernels for 1%

commit v1 on v0

--- a/solution.py
+++ b/solution.py
@@ -16,25 +16,30 @@
 DMA = pltpu.SemaphoreType.DMA
 
 
-def call(kernel, out_shape, in_specs, scratch=(), flops=0, moved=0):
+def call(kernel, out_shape, in_specs, scratch=(), flops=0, moved=0, limit=32):
     return pl.pallas_call(
         kernel,
         out_shape=out_shape,
         in_specs=in_specs,
         out_specs=jax.tree.map(lambda _: VMEM, out_shape),
         scratch_shapes=list(scratch),
-        compiler_params=pltpu.CompilerParams(vmem_limit_bytes=32 * 2**20),
+        compiler_params=pltpu.CompilerParams(vmem_limit_bytes=limit * 2**20),
         cost_estimate=pl.CostEstimate(flops=flops, bytes_accessed=moved, transcendentals=0),
     )
 
 
 def take_half(amp, out, token, sem):
-    half = out.shape[1]
-    offset = pl.multiple_of((1 - lax.axis_index("yl")) * half, half)
-    copy = pltpu.make_async_copy(amp.at[0, :, pl.ds(offset, half)], out, sem)
-    copy.start()
+    rows, half = out.shape
+    columns = pl.ds(pl.multiple_of((1 - lax.axis_index("yl")) * half, half), half)
+    copies = []
+    for i in range(4):
+        some = pl.ds(i * rows // 4, rows // 4)
+        copies.append(pltpu.make_async_copy(amp.at[0, some, columns], out.at[some], sem.at[i]))
+    for copy in copies:
+        copy.start()
     token[...] = jnp.zeros_like(token)
-    copy.wait()
+    for copy in copies:
+        copy.wait()
 
 
 def take_late(sib_low, sib_high, early, away, out):
@@ -103,8 +108,9 @@
             jax.ShapeDtypeStruct((8, 128), jnp.float32),
         ),
         [HBM],
-        [DMA],
+        [pltpu.SemaphoreType.DMA((4,))],
         moved=4 * rows * half,
+        limit=52,
     )(amplitudes)
     early = lax.ppermute(away, OCC, [(0, 2), (2, 0)])
     depth_own, width_all = integrals.shape[1:]

time: 74.8 us -> 74.5 us (level)
  local copies, waits for them, and re-layouts: 2.28 us -> 0.61 us
  Pallas kernels: 1.77 us -> 3.01 us
    unnamed x7 -> x5, local copies, waits for them, and re-layouts: 2.28 us -> 0.6 us
    pallas_call x1, Pallas kernels: 0.09 us -> 1.33 us  [per_device(): call(take_half, (jax.ShapeDtypeStruct((rows, half), jnp.bfloat16), jax.Sh...]
where the time goes in v1:
time: 74.5 us; the launch traced here: 74.2 us
  blocking collectives  38.1 us (51%)
  starting transfers between devices  18.3 us (25%)
  waiting for transfers between devices  13.3 us (18%)
  Pallas kernels  3.01 us (4%)
  between operations  0.77 us (1%)
    all_to_all x1, blocking collectives, per_device(): plane = lax.all_to_all(plane, 'z', split_axis=0, concat_axis=0, tiled=True)  25.3 us
    all_to_all x1, blocking collectives, per_device(): lax.all_to_all(parts, ('x', 'yh', 'yl'), split_axis=0, concat_axis=0, til...  12.8 us
    ppermute x1, starting transfers between devices, per_device(): sib_low = lax.ppermute(own_low, 'core', SWAP)  10.1 us
    ppermute x1, waiting for transfers between devices, per_device(): late = lax.ppermute(away_late, OCC, [(1, 3), (3, 1)])  8.48 us
    ppermute x1, starting transfers between devices, per_device(): late = lax.ppermute(away_late, OCC, [(1, 3), (3, 1)])  3.64 us
    ppermute x1, waiting for transfers between devices, per_device(): return lax.ppermute(block, ('x', 'core'), swap)  3 us
    ppermute x1, starting transfers between devices, per_device(): sib_high = lax.ppermute(own_high, 'core', SWAP)  1.92 us
    ppermute x1, starting transfers between devices, per_device(): return lax.ppermute(block, ('x', 'core'), swap)  1.92 us
  transfers between devices with their start and end apart: 5, of which 3 were waited for; matrix products, arithmetic and copies ran while one was open for 0% of the time, Pallas kernels for 1%

profile of v1, /device:TPU:1, one launch (start us, length us, event | category | flops | bytes accessed | tf_op | source)
XLA Modules:
  0.0 74.2 jit_solution(17467085066995906215)
XLA Ops:
  0.0 0.0 copy-start.1
  0.0 1.3 %shard_map.37 = (bf16[192,2048]{1,0:T(8,128)(2,1)S(1)}, f32[8,128]{1,0:T(8,128)S(1)}) custom-call(bf16[1,192,4096]{2,1,0:T(8,128)(2,1)} %amp.3), custom_call_target="tpu_custom_call" | custom-call | bytes 1572864 | tf_op jit(solution)/shard_map/pallas_call | solution.py:104
  1.3 0.7 collective-permute-start
  2.1 0.0 copy-done.1
  2.1 0.0 copy-start
  2.1 0.1 shard_map.38
  2.2 10.1 %collective-permute-start.1 = (bf16[512,512]{1,0:T(8,128)(2,1)S(1)}, bf16[512,512]{1,0:T(8,128)(2,1)S(1)}, u32[]{:S(2)}, u32[]{:S(2)}) collective-permute-start(bf16[512,512]{1,0:T(8,128)(2,1)S(1)} %get-tuple-element.13.own_low), channel_id=1, source_target_pairs={{0,1},{1,0},{2,3},{3,2},{4,5},{5,4},{6,7},{7,6},{8,9},{9,8},{10,11... | collective-permute-start | bytes 1572872 | tf_op jit(solution)/shard_map/ppermute | solution.py:121
  12.3 1.9 %collective-permute-start.2 = (bf16[512,512]{1,0:T(8,128)(2,1)S(1)}, bf16[512,512]{1,0:T(8,128)(2,1)S(1)}, u32[]{:S(2)}, u32[]{:S(2)}) collective-permute-start(bf16[512,512]{1,0:T(8,128)(2,1)S(1)} %get-tuple-element.14.own_high), channel_id=1, source_target_pairs={{0,1},{1,0},{2,3},{3,2},{4,5},{5,4},{6,7},{7,6},{8,9},{9,8},{10,11... | collective-permute-start | bytes 1572872 | tf_op jit(solution)/shard_map/ppermute | solution.py:122
  14.2 0.0 collective-permute-done.1.sib_low
  14.2 1.9 %collective-permute-done.2.sib_high = bf16[512,512]{1,0:T(8,128)(2,1)S(1)} collective-permute-done((bf16[512,512]{1,0:T(8,128)(2,1)S(1)}, bf16[512,512]{1,0:T(8,128)(2,1)S(1)}, u32[]{:S(2)}, u32[]{:S(2)}) %collective-permute-start.2) | collective-permute-done | bytes 524320 | tf_op jit(solution)/shard_map/ppermute | solution.py:122
  16.1 0.0 collective-permute-done.early
  16.1 0.1 shard_map.39
  16.2 3.6 %collective-permute-start.3 = (bf16[192,2048]{1,0:T(8,128)(2,1)S(1)}, bf16[192,2048]{1,0:T(8,128)(2,1)S(1)}, u32[]{:S(2)}, u32[]{:S(2)}) collective-permute-start(bf16[192,2048]{1,0:T(8,128)(2,1)S(1)} %shard_map.39), channel_id=1, source_target_pairs={{1,3},{3,1},{5,7},{7,5},{9,11},{11,9},{13,15},{15,13},{17,19},{19,... | collective-permute-start | bytes 2359304 | tf_op jit(solution)/shard_map/ppermute | solution.py:137
  20.5 0.0 copy-done
  20.5 0.9 %shard_map.40 = (f32[2,2,2,96,128]{4,3,2,1,0:T(8,128)S(1)}, bf16[2048,512]{1,0:T(8,128)(2,1)S(1)}) custom-call(s32[1]{0:T(128)S(6)} %copy.5.mask, bf16[1,192,4096]{2,1,0:T(8,128)(2,1)S(1)} %copy-done, bf16[512,512]{1,0:T(8,128)(2,1)S(1)} %get-tuple-element.13.own_low, bf16[512,512]{1,0:T(8,128)(2,1)S(1)} %get-tuple-element.14.own_high, ...), custom_call_target="tpu_custom_call" | custom-call | flops 1 | bytes 1 | tf_op jit(solution)/shard_map/pallas_call | solution.py:126
  21.4 8.5 %collective-permute-done.3.late = bf16[192,2048]{1,0:T(8,128)(2,1)S(1)} collective-permute-done((bf16[192,2048]{1,0:T(8,128)(2,1)S(1)}, bf16[192,2048]{1,0:T(8,128)(2,1)S(1)}, u32[]{:S(2)}, u32[]{:S(2)}) %collective-permute-start.3) | collective-permute-done | bytes 786464 | tf_op jit(solution)/shard_map/ppermute | solution.py:137
  29.8 0.7 shard_map.41
  30.5 12.8 %all_to_all.10 = f32[16,96,128]{2,1,0:T(8,128)S(1)} all-to-all(f32[16,96,128]{2,1,0:T(8,128)S(1)} %bitcast.2), channel_id=1, replica_groups=mesh['x'=4,'z'=16,'yh'=2,'yl'=2,'core'=2] {'x','yh','yl'}, dimensions={0} | all-to-all | bytes 1572864 | tf_op jit(solution)/shard_map/all_to_all | solution.py:148
  43.3 25.3 %all_to_all.11 = f32[16,6,128]{2,1,0:T(8,128)S(1)} all-to-all(f32[16,6,128]{2,1,0:T(8,128)S(1)} %reshape.7), channel_id=1, replica_groups=mesh['x'=4,'z'=16,'yh'=2,'yl'=2,'core'=2] {'z'}, dimensions={0} | all-to-all | bytes 98304 | tf_op jit(solution)/shard_map/all_to_all | solution.py:150
  68.7 1.9 %collective-permute-start.4 = (f32[6,128]{1,0:T(8,128)S(1)}, f32[6,128]{1,0:T(8,128)S(1)}, u32[]{:S(2)}, u32[]{:S(2)}) collective-permute-start(f32[6,128]{1,0:T(8,128)S(1)} %reduce_sum.19), channel_id=1, source_target_pairs={{0,0},{1,128},{128,1},{129,129},{256,256},{257,384},{384,257},{385... | collective-permute-start | bytes 9224 | tf_op jit(solution)/shard_map/ppermute | solution.py:153
  70.6 3.0 %collective-permute-done.4 = f32[6,128]{1,0:T(8,128)S(1)} collective-permute-done((f32[6,128]{1,0:T(8,128)S(1)}, f32[6,128]{1,0:T(8,128)S(1)}, u32[]{:S(2)}, u32[]{:S(2)}) %collective-permute-start.4) | collective-permute-done | bytes 3104 | tf_op jit(solution)/shard_map/ppermute | solution.py:153
  73.6 0.6 copy.6
  (3 shorter events, 0.1 us)
Async XLA Ops:
  0.0 2.1 %copy-start.1 = (bf16[1,1024,512]{2,1,0:T(8,128)(2,1)S(1)}, bf16[1,1024,512]{2,1,0:T(8,128)(2,1)}, u32[]{:S(2)}) copy-start(bf16[1,1024,512]{2,1,0:T(8,128)(2,1)} %param.4) | copy-start | bytes 3145732
  1.3 14.8 %collective-permute-start = (bf16[192,2048]{1,0:T(8,128)(2,1)S(1)}, bf16[192,2048]{1,0:T(8,128)(2,1)S(1)}, u32[]{:S(2)}, u32[]{:S(2)}) collective-permute-start(bf16[192,2048]{1,0:T(8,128)(2,1)S(1)} %get-tuple-element.11.away), channel_id=1, source_target_pairs={{0,2},{2,0},{4,6},{6,4},{8,10},{10,8},{12,14},{14,12},{16,18},{18,... | collective-permute-start | bytes 2359304 | tf_op jit(solution)/shard_map/ppermute | solution.py:115
  2.1 18.4 %copy-start = (bf16[1,192,4096]{2,1,0:T(8,128)(2,1)S(1)}, bf16[1,192,4096]{2,1,0:T(8,128)(2,1)}, u32[]{:S(2)}) copy-start(bf16[1,192,4096]{2,1,0:T(8,128)(2,1)} %amp.3) | copy-start | bytes 4718596
  2.2 12.1 %collective-permute-start.1 = (bf16[512,512]{1,0:T(8,128)(2,1)S(1)}, bf16[512,512]{1,0:T(8,128)(2,1)S(1)}, u32[]{:S(2)}, u32[]{:S(2)}) collective-permute-start(bf16[512,512]{1,0:T(8,128)(2,1)S(1)} %get-tuple-element.13.own_low), channel_id=1, source_target_pairs={{0,1},{1,0},{2,3},{3,2},{4,5},{5,4},{6,7},{7,6},{8,9},{9,8},{10,11... | collective-permute-start | bytes 1572872 | tf_op jit(solution)/shard_map/ppermute | solution.py:121
  12.3 3.8 %collective-permute-start.2 = (bf16[512,512]{1,0:T(8,128)(2,1)S(1)}, bf16[512,512]{1,0:T(8,128)(2,1)S(1)}, u32[]{:S(2)}, u32[]{:S(2)}) collective-permute-start(bf16[512,512]{1,0:T(8,128)(2,1)S(1)} %get-tuple-element.14.own_high), channel_id=1, source_target_pairs={{0,1},{1,0},{2,3},{3,2},{4,5},{5,4},{6,7},{7,6},{8,9},{9,8},{10,11... | collective-permute-start | bytes 1572872 | tf_op jit(solution)/shard_map/ppermute | solution.py:122
  16.2 13.7 %collective-permute-start.3 = (bf16[192,2048]{1,0:T(8,128)(2,1)S(1)}, bf16[192,2048]{1,0:T(8,128)(2,1)S(1)}, u32[]{:S(2)}, u32[]{:S(2)}) collective-permute-start(bf16[192,2048]{1,0:T(8,128)(2,1)S(1)} %shard_map.39), channel_id=1, source_target_pairs={{1,3},{3,1},{5,7},{7,5},{9,11},{11,9},{13,15},{15,13},{17,19},{19,... | collective-permute-start | bytes 2359304 | tf_op jit(solution)/shard_map/ppermute | solution.py:137
  68.7 4.9 %collective-permute-start.4 = (f32[6,128]{1,0:T(8,128)S(1)}, f32[6,128]{1,0:T(8,128)S(1)}, u32[]{:S(2)}, u32[]{:S(2)}) collective-permute-start(f32[6,128]{1,0:T(8,128)S(1)} %reduce_sum.19), channel_id=1, source_target_pairs={{0,0},{1,128},{128,1},{129,129},{256,256},{257,384},{384,257},{385... | collective-permute-start | bytes 9224 | tf_op jit(solution)/shard_map/ppermute | solution.py:153
